TPU v7x, 32 devices: a whole 2x2x4 slice. The times are simulated.
32 devices in a mesh: modes: 16 (over z, y, x), grp: 2 (over core).
Axes of the slice: x: 2, y: 2, z: 4, core: 2. Of those that a mesh axis runs over, the one named last changes fastest.
Arguments:
- left_core: bfloat16 [32768, 512], P(('modes', 'grp')), may hold values from -6 to 6
- right_core: bfloat16 [32768, 512], P(('modes', 'grp')), may hold values from -6 to 6
- gauss_core: bfloat16 [32768, 256], P(('modes', 'grp')), may hold values from -0.03125 to 0.03125
Outputs:
- left_new: bfloat16 [32768, 256], P(('modes', 'grp'))
- right_new: bfloat16 [32768, 256], P(('modes', 'grp'))
All inputs are finite; a program needn't handle non-finite values.
Results may differ from a plain program's by a relative error of at most 0.0012.
Values sent between devices are 32-bit elements; how exact they have to be, the bound alone decides.
A program may use at most 64 MiB of HBM per device.

v0:
```python
import math

import jax
import jax.numpy as jnp
from jax import lax
from jax.sharding import PartitionSpec as P


def contract_rows(first, second, precision=None):
    return lax.dot_general(
        first,
        second,
        (((0,), (0,)), ((), ())),
        precision=precision,
        preferred_element_type=jnp.float32,
    )


def local(left_core, right_core, gauss_core):
    high = lax.Precision.HIGHEST
    local_rows = left_core.shape[0]
    devices = lax.axis_size("modes") * lax.axis_size("grp")
    norm_scale = math.sqrt(local_rows * devices)
    sketch_part = contract_rows(right_core, gauss_core)
    left_gram = contract_rows(left_core, left_core)
    sketch, left_gram = lax.psum((sketch_part, left_gram), ("modes", "grp"))
    tall_sketch = jnp.dot(left_core, sketch, precision=high, preferred_element_type=jnp.float32)
    cross_gram = contract_rows(sketch, left_gram, high)
    gram = jnp.dot(cross_gram, sketch, precision=high)
    chol_lower = jnp.linalg.cholesky(gram)
    q_trans = jax.scipy.linalg.solve_triangular(chol_lower, tall_sketch.T, lower=True)
    projected = jax.scipy.linalg.solve_triangular(chol_lower, cross_gram, lower=True)
    left_new = (q_trans.T * norm_scale).astype(jnp.bfloat16)
    right_new = jnp.dot(
        right_core, (projected / norm_scale).T, precision=high, preferred_element_type=jnp.float32
    ).astype(jnp.bfloat16)
    return (left_new, right_new)


def solution(mesh):
    return jax.shard_map(
        local,
        mesh=mesh,
        in_specs=(P(("modes", "grp"), None), P(("modes", "grp"), None), P(("modes", "grp"), None)),
        out_specs=(P(("modes", "grp"), None), P(("modes", "grp"), None)),
        check_vma=False,
    )
```

profile of v0, /device:TPU:0, one launch (start us, length us, event | category | flops | bytes accessed | tf_op | source)
XLA Modules:
  0.0 226.9 jit_solution(11314075642952653872)
XLA Ops:
  7.2 0.0 copy-start
  7.2 0.0 copy-start.2
  7.2 0.0 copy-start.5
  7.2 0.0 all-reduce.4.cloned.1.call-start
  7.2 1.1 copy-done
  8.4 1.8 fusion.22
  10.2 0.0 copy-done.2
  10.2 0.0 copy-done.5
  10.2 1.3 fusion.21
  11.4 0.0 all-reduce.4.cloned.1.call-update
  11.5 137.7 %all-reduce.4.cloned.1.call-done = (f32[512,256]{1,0:T(8,128)}, f32[512,512]{1,0:T(8,128)}) async-done(((f32[512,256]{1,0:T(8,128)}, f32[512,512]{1,0:T(8,128)}), (f32[512,256]{1,0:T(8,128)}, f32[512,512]{1,0:T(8,128)})) %all-reduce.4.cloned.1.call-update) | async-done | bytes 1572880 | tf_op jit(solution)/shard_map/psum | solution.py:26
  149.1 0.0 copy-start.1
  149.1 0.0 copy-start.4
  149.1 3.0 %fusion.25 = f32[256,1024]{1,0:T(8,128)S(1)} fusion(f32[512,256]{1,0:T(8,128)} %get-tuple-element.20, bf16[1024,512]{1,0:T(8,128)(2,1)S(1)} %copy-done), kind=kOutput, calls=%fused_computation.48 | convolution fusion | flops 1610612736 | bytes 2621440 | tf_op jit(solution)/shard_map/dot_general | solution.py:27
  152.1 0.0 copy-done.1
  152.2 0.0 copy-done.4
  152.2 1.1 fusion.23
  153.2 0.6 fusion.24
  153.8 0.1 copy.5
  154.0 11.7 %cholesky.50 = f32[128,128]{1,0:T(8,128)S(1)} custom-call(f32[128,128]{1,0:T(8,128)S(1)} %cholesky.118), custom_call_target="Cholesky" | custom-call | tf_op jit(solution)/shard_map/jit(cholesky)/cholesky | solution.py:30
  165.8 9.8 %custom-call.18 = f32[1,128,128]{1,2,0:T(8,128)S(1)} custom-call(f32[1,128,128]{2,1,0:T(8,128)S(1)} %get-tuple-element.27), custom_call_target="InvertDiagBlocksLowerTriangular" | custom-call | tf_op jit(solution)/shard_map/jit(cholesky)/cholesky | solution.py:30
  175.6 0.2 constant_dynamic-update-slice_fusion.1
  175.8 0.3 convolution_subtract_fusion.2
  176.1 11.9 %cholesky.105 = f32[128,128]{1,0:T(8,128)S(1)} custom-call(f32[128,128]{1,0:T(8,128)S(1)} %convolution_subtract_fusion.2), custom_call_target="Cholesky" | custom-call | tf_op jit(solution)/shard_map/jit(cholesky)/cholesky | solution.py:30
  188.0 0.7 compare_reduce_fusion
  190.1 0.1 triangular_solve.72
  190.1 4.0 %while.1 = (s32[]{:T(128)}, f32[256,256]{1,0:T(8,128)S(1)}, s32[2,2]{1,0:T(2,128)S(1)}, f32[2,128,128]{2,1,0:T(8,128)S(1)}, s32[]{:T(128)}) while((s32[]{:T(128)}, f32[256,256]{1,0:T(8,128)S(1)}, s32[2,2]{1,0:T(2,128)S(1)}, f32[2,128,128]{2,1,0:T(8,128)S(1)}, s32[]{:T(128)}) %tuple.28), condition=%wide.while_cond, body=%wide.while_body.sunk | while | flops 2 | bytes 131181 | solution.py:31
  190.1 0.6 fusion.44
  190.7 1.4 bitcast_dynamic-update-slice_fusion.2
  192.1 0.6 fusion.44
  192.7 1.4 bitcast_dynamic-update-slice_fusion.2
  194.1 19.7 %custom-call.19 = f32[2,128,128]{1,2,0:T(8,128)S(1)} custom-call(f32[2,128,128]{2,1,0:T(8,128)S(1)} %get-tuple-element.9), custom_call_target="InvertDiagBlocksLowerTriangular" | custom-call | tf_op jit(solution)/shard_map/jit(_solve_triangular)/triangular_solve | solution.py:31
  213.8 0.0 copy-start.3
  213.8 0.4 fusion.7
  214.2 0.4 convolution_subtract_fusion.1
  214.6 0.4 fusion.14
  215.0 0.0 copy-done.3
  215.0 1.0 fusion
  216.1 1.0 copy.7
  217.1 0.6 fusion.3
  217.7 0.6 convolution_subtract_fusion
  218.3 0.6 fusion.15
  218.9 0.1 fusion.2
  219.0 1.0 copy.6
  (10 shorter events, 0.2 us)
Async XLA Ops:
  7.2 1.2 copy-start
  7.2 3.0 %copy-start.2 = (bf16[1024,512]{1,0:T(8,128)(2,1)S(1)}, bf16[1024,512]{1,0:T(8,128)(2,1)}, u32[]{:S(2)}) copy-start(bf16[1024,512]{1,0:T(8,128)(2,1)} %param.4) | copy-start | bytes 3145732
  7.2 3.0 %copy-start.5 = (bf16[1024,256]{1,0:T(8,128)(2,1)S(1)}, bf16[1024,256]{1,0:T(8,128)(2,1)}, u32[]{:S(2)}) copy-start(bf16[1024,256]{1,0:T(8,128)(2,1)} %param.5) | copy-start | bytes 1572868
  7.2 141.9 %all-reduce.4.cloned.1.call-start = ((), (), s32[]{:S(2)}) async-start(), calls=%async_computation | async-start | bytes 3145728 | tf_op jit(solution)/shard_map/psum | solution.py:26
  149.1 3.0 %copy-start.1 = (f32[512,256]{1,0:T(8,128)S(1)}, f32[512,256]{1,0:T(8,128)}, u32[]{:S(2)}) copy-start(f32[512,256]{1,0:T(8,128)} %get-tuple-element.20) | copy-start | bytes 1572868
  149.1 3.0 %copy-start.4 = (f32[512,512]{1,0:T(8,128)S(1)}, f32[512,512]{1,0:T(8,128)}, u32[]{:S(2)}) copy-start(f32[512,512]{1,0:T(8,128)} %get-tuple-element.21) | copy-start | bytes 3145732
  213.8 1.2 copy-start.3
Sparse Core Ops, SparseCore 0:
  14.1 134.9 all-reduce.3
where the time goes:
time: 227 us
  waiting for transfers between devices  138 us (61%)
  other arithmetic  54 us (24%)
  between operations  15.5 us (7%)
  matrix products  12.2 us (5%)
  local copies, waits for them, and re-layouts  7.33 us (3%)
    psum x1, waiting for transfers between devices, local(): sketch, left_gram = lax.psum((sketch_part, left_gram), ('modes', 'grp'))  138 us
    another operation x6, other arithmetic, local(): chol_lower = jnp.linalg.cholesky(gram)  34.2 us
    another operation x3, other arithmetic, local(): jax.scipy.linalg.solve_triangular(chol_lower, tall_sketch.T, lower=True)  19.7 us
  transfers between devices with their start and end apart: 1, of which 1 were waited for; matrix products, arithmetic and copies ran while one was open for 0% of the time, Pallas kernels for 0%

commit v1 on v0

v1 whole, which is shorter than its diff:
```python
import functools
import math

import jax
import jax.numpy as jnp
from jax import lax
from jax.experimental import pallas as pl
from jax.experimental.pallas import tpu as pltpu
from jax.sharding import PartitionSpec as P

MESH = pl.DeviceIdType.MESH
F32 = jnp.float32
BF16 = jnp.bfloat16
B = 128
T = 8


def dot(a, b, dims, precision=None):
    return lax.dot_general(a, b, (dims, ((), ())), precision=precision, preferred_element_type=F32)


def block_list(rank, target):
    n, k = rank // B, target // B
    sketch = [(0, i, j) for i in range(n) for j in range(k)]
    gram = [(1, i, j) for i in range(n) for j in range(i, n)]
    return sketch + gram


def plan(rank, target, modes):
    devices = 2 * modes
    rows = len(block_list(rank, target)) * B
    tiles = -(-rows // (devices * T))
    a = -(-tiles // 2) * T
    b = tiles * T - a
    return a, b, (a + b) * devices


def reduce_kernel(modes, a, b, left, right, gauss, full, buf, r_core, ra1, rb1, ra2, rb2, rza, rzb, ssem, rsem, zsend, zrecv):
    nz = modes // 4
    m, c = lax.axis_index("modes"), lax.axis_index("grp")
    x, y, z = m % 2, (m // 2) % 2, m // 4
    core = (m, 1 - c)
    xp = (m + 1 - 2 * x, c)
    yp = (m + 2 - 4 * y, c)
    zs = [((z + k) % nz) for k in range(1, nz)]
    zp = [(x + 2 * y + 4 * t, c) for t in zs]

    barrier = pltpu.get_barrier_semaphore()
    partners = [core, xp, yp] + zp
    for p in partners:
        pl.semaphore_signal(barrier, inc=1, device_id=p, device_id_type=MESH)

    rank, target = right.shape[1], gauss.shape[1]
    n, kb = rank // B, target // B
    pos = 0
    for i in range(n):
        s = dot(right[:, i * B:(i + 1) * B], gauss[...], ((0,), (0,)))
        for j in range(kb):
            buf[pos * B:(pos + 1) * B, :] = s[:, j * B:(j + 1) * B]
            pos += 1
    for i in range(n):
        g = dot(left[:, i * B:(i + 1) * B], left[:, i * B:], ((0,), (0,)))
        for j in range(n - i):
            buf[pos * B:(pos + 1) * B, :] = g[:, j * B:(j + 1) * B]
            pos += 1
    total = buf.shape[0]
    if pos * B < total:
        buf[pos * B:, :] = jnp.zeros((total - pos * B, B), F32)

    pl.semaphore_wait(barrier, len(partners))

    half = total // 2
    qa, qb = nz * a, nz * b
    base_a = c * half
    base_b = base_a + 4 * qa

    def at(ref, start, size):
        return ref.at[pl.ds(pl.multiple_of(start, T), size), :]

    def send(src, dst, k, dev):
        cp = pltpu.make_async_remote_copy(
            src_ref=src, dst_ref=dst, send_sem=ssem.at[k], recv_sem=rsem.at[k], device_id=dev, device_id_type=MESH)
        cp.start()
        return cp

    def add(start, size, other):
        i = pl.ds(pl.multiple_of(start, T), size)
        buf[i, :] = buf[i, :] + other[...]

    cp = send(at(buf, (1 - c) * half, half), r_core, 0, core)
    cp.wait()
    add(base_a, half, r_core)

    a1, b1 = base_a + x * 2 * qa, base_b + y * 2 * qb
    cps = [send(at(buf, base_a + (1 - x) * 2 * qa, 2 * qa), ra1, 1, xp)]
    if b:
        cps.append(send(at(buf, base_b + (1 - y) * 2 * qb, 2 * qb), rb1, 2, yp))
    cps[0].wait()
    add(a1, 2 * qa, ra1)
    if b:
        cps[1].wait()
        add(b1, 2 * qb, rb1)
    a2, b2 = a1 + y * qa, b1 + x * qb
    cps = [send(at(buf, a1 + (1 - y) * qa, qa), ra2, 3, yp)]
    if b:
        cps.append(send(at(buf, b1 + (1 - x) * qb, qb), rb2, 4, xp))
    cps[0].wait()
    add(a2, qa, ra2)
    if b:
        cps[1].wait()
        add(b2, qb, rb2)

    def zsends(src, dst_a, dst_b, phase):
        cps = []
        for k in range(nz - 1):
            for part, base, size, dst in ((0, a2, a, dst_a), (1, b2, b, dst_b)):
                if not size:
                    continue
                where = zs[k] if phase == 0 else z
                source = at(src, base + where * size, size)
                target_ref = dst.at[k] if phase == 0 else source
                cp = pltpu.make_async_remote_copy(
                    src_ref=source, dst_ref=target_ref, send_sem=zsend.at[phase, part, k],
                    recv_sem=zrecv.at[phase, part, k], device_id=zp[k], device_id_type=MESH)
                cp.start()
                cps.append(cp)
        for cp in cps:
            cp.wait()

    zsends(buf, rza, rzb, 0)
    for base, size, got in ((a2, a, rza), (b2, b, rzb)):
        if size:
            i = pl.ds(pl.multiple_of(base + z * size, T), size)
            acc = buf[i, :]
            for k in range(nz - 1):
                acc = acc + got[k]
            full[i, :] = acc

    zsends(full, full, full, 1)
    cps = [send(at(full, a2, qa), at(full, a2, qa), 5, yp)]
    if b:
        cps.append(send(at(full, b2, qb), at(full, b2, qb), 6, xp))
    for cp in cps:
        cp.wait()
    cps = [send(at(full, a1, 2 * qa), at(full, a1, 2 * qa), 7, xp)]
    if b:
        cps.append(send(at(full, b1, 2 * qb), at(full, b1, 2 * qb), 8, yp))
    for cp in cps:
        cp.wait()
    send(at(full, base_a, half), at(full, base_a, half), 9, core).wait()


def reduced(left, right, gauss):
    modes = lax.axis_size("modes")
    a, b, total = plan(right.shape[1], gauss.shape[1], modes)
    nz = modes // 4
    bb = max(b, T)
    dma = pltpu.SemaphoreType.DMA
    return pl.pallas_call(
        functools.partial(reduce_kernel, modes, a, b),
        out_shape=jax.ShapeDtypeStruct((total, B), F32),
        in_specs=[pl.BlockSpec(memory_space=pltpu.VMEM)] * 3,
        out_specs=pl.BlockSpec(memory_space=pltpu.VMEM),
        scratch_shapes=[
            pltpu.VMEM((total, B), F32),
            pltpu.VMEM((total // 2, B), F32),
            pltpu.VMEM((2 * nz * a, B), F32),
            pltpu.VMEM((2 * nz * bb, B), F32),
            pltpu.VMEM((nz * a, B), F32),
            pltpu.VMEM((nz * bb, B), F32),
            pltpu.VMEM((nz - 1, a, B), F32),
            pltpu.VMEM((nz - 1, bb, B), F32),
            dma((10,)),
            dma((10,)),
            dma((2, 2, nz - 1)),
            dma((2, 2, nz - 1)),
        ],
        compiler_params=pltpu.CompilerParams(collective_id=0, has_side_effects=True, vmem_limit_bytes=40 << 20),
    )(left, right, gauss)


def factor_inverse(block, spl, rowbuf):
    n = B // T
    row = lax.broadcasted_iota(jnp.int32, (T, B), 0)
    lane = lax.broadcasted_iota(jnp.int32, (T, B), 1)
    A = [block[t * T:(t + 1) * T, :] for t in range(n)]
    M = [(row + t * T == lane).astype(F32) for t in range(n)]
    out = []
    for p in range(n):
        k0 = p * T
        for j in range(T):
            spl[p % 2, j] = jnp.broadcast_to(A[p][:, k0 + j:k0 + j + 1], (T, B))
        s = [[jnp.broadcast_to(spl[p % 2, j, i:i + 1, :], (T, B)) if j <= i else None for j in range(T)] for i in range(T)]
        w = [[None] * T for _ in range(T)]
        rs, rd = [], []
        for k in range(T):
            r = lax.rsqrt(s[k][k])
            rs.append(r)
            rd.append(r * r)
            for i in range(k + 1, T):
                w[i][k] = s[i][k] * rd[k]
            for j in range(k + 1, T):
                for i in range(j, T):
                    s[i][j] = s[i][j] - w[i][k] * s[j][k]
        rowbuf[p % 2, 0] = A[p]
        rowbuf[p % 2, 1] = M[p]
        xa = [jnp.broadcast_to(rowbuf[p % 2, 0, i:i + 1, :], (T, B)) for i in range(T)]
        xm = [jnp.broadcast_to(rowbuf[p % 2, 1, i:i + 1, :], (T, B)) for i in range(T)]
        for k in range(T):
            for i in range(k + 1, T):
                xa[i] = xa[i] - w[i][k] * xa[k]
                xm[i] = xm[i] - w[i][k] * xm[k]
        o = xm[0] * rs[0]
        for i in range(1, T):
            o = jnp.where(row == i, xm[i] * rs[i], o)
        out.append(o)
        if p + 1 == n:
            break
        va = [xa[i] * rd[i] for i in range(T)]
        vm = [xm[i] * rd[i] for i in range(T)]
        for k in range(T - 1, 0, -1):
            for i in range(k):
                va[i] = va[i] - w[k][i] * va[k]
                vm[i] = vm[i] - w[k][i] * vm[k]
        for t in range(p + 1, n):
            da = dm = None
            for j in range(T):
                cj = jnp.broadcast_to(A[t][:, k0 + j:k0 + j + 1], (T, B))
                da = cj * va[j] if da is None else da + cj * va[j]
                dm = cj * vm[j] if dm is None else dm + cj * vm[j]
            A[t] = A[t] - da
            M[t] = M[t] - dm
    return jnp.concatenate(out, axis=0)


def halves(v):
    hi = v.astype(BF16)
    return hi, (v - hi.astype(F32)).astype(BF16)


def solve_kernel(scale, full, left, right, left_new, right_new, sk, gm, spl, rowbuf):
    high = lax.Precision.HIGHEST
    rank, target = left.shape[1], left_new.shape[1]
    for pos, (kind, i, j) in enumerate(block_list(rank, target)):
        v = full[pos * B:(pos + 1) * B, :]
        if kind == 0:
            sk[j * B:(j + 1) * B, i * B:(i + 1) * B] = v.T
        else:
            gm[i * B:(i + 1) * B, j * B:(j + 1) * B] = v
            if i != j:
                gm[j * B:(j + 1) * B, i * B:(i + 1) * B] = v.T
    nn, nt = ((1,), (0,)), ((1,), (1,))
    st = sk[...]
    cross = dot(st, gm[...], nn, high)
    gram = dot(cross, st, nt, high)
    nb = target // B
    low, inv = [], []
    for r in range(nb):
        diag = gram[r * B:(r + 1) * B, r * B:(r + 1) * B]
        if r:
            prev = inv[0] if r == 1 else jnp.concatenate(inv, axis=0)
            lr = dot(gram[r * B:(r + 1) * B, :r * B], prev, nt, high)
            diag = diag - dot(lr, lr, nt, high)
        mi = factor_inverse(diag, spl, rowbuf)
        if r:
            rest = -dot(mi, dot(lr, prev, nn, high), nn, high)
            mi = jnp.concatenate([rest, mi], axis=1)
            inv = [jnp.concatenate([v, jnp.zeros((B, B), F32)], axis=1) for v in inv]
        inv.append(mi)
    inverse = inv[0] if nb == 1 else jnp.concatenate(inv, axis=0)
    wh, wl = halves(dot(inverse, st, nn, high) * scale)
    ph, plo = halves(dot(inverse, cross, nn, high) * (1.0 / scale))
    left_new[...] = (dot(left[...], wh, nt) + dot(left[...], wl, nt)).astype(BF16)
    right_new[...] = (dot(right[...], ph, nt) + dot(right[...], plo, nt)).astype(BF16)


def local(left_core, right_core, gauss_core):
    rows, rank = left_core.shape
    target = gauss_core.shape[1]
    devices = lax.axis_size("modes") * lax.axis_size("grp")
    full = reduced(left_core, right_core, gauss_core)
    out = jax.ShapeDtypeStruct((rows, target), BF16)
    return pl.pallas_call(
        functools.partial(solve_kernel, math.sqrt(rows * devices)),
        out_shape=(out, out),
        in_specs=[pl.BlockSpec(memory_space=pltpu.VMEM)] * 3,
        out_specs=(pl.BlockSpec(memory_space=pltpu.VMEM),) * 2,
        scratch_shapes=[
            pltpu.VMEM((target, rank), F32),
            pltpu.VMEM((rank, rank), F32),
            pltpu.VMEM((2, T, T, B), F32),
            pltpu.VMEM((2, 2, T, B), F32),
        ],
        compiler_params=pltpu.CompilerParams(vmem_limit_bytes=40 << 20),
    )(full, left_core, right_core)


def solution(mesh):
    spec = P(("modes", "grp"), None)
    return jax.shard_map(local, mesh=mesh, in_specs=(spec,) * 3, out_specs=(spec, spec), check_vma=False)
```

time: 227 us -> 54.4 us (0.24)
  waiting for transfers between devices: 138 us -> 0 us
  other arithmetic: 54 us -> 0 us
  Pallas kernels: 0 us -> 50.1 us
  between operations: 15.5 us -> 0.65 us
  matrix products: 12.2 us -> 0 us
  local copies, waits for them, and re-layouts: 7.33 us -> 3.48 us
    psum x1 -> x0, waiting for transfers between devices: 138 us -> none  [local(): sketch, left_gram = lax.psum((sketch_part, left_gram), ('modes', 'grp'))]
    another operation x9 -> x0, other arithmetic: 53.9 us -> none  [the longest x6 34.2 us: local(): chol_lower = jnp.linalg.cholesky(gram)]
    pallas_call x0 -> x2, Pallas kernels: none -> 50.1 us  [the longest x1 35.9 us: reduced(): pl.pallas_call(functools.partial(reduce_kernel, modes, a, b), out_shape=j...]
    dot_general x6 -> x0, matrix products: 8.7 us -> none  [the longest x3 4.09 us: contract_rows(): lax.dot_general(first, second, (((0,), (0,)), ((), ())), precision=precis...]
    another operation x9 -> x0, local copies, waits for them, and re-layouts: 4.02 us -> none
    another operation x8 -> x0, matrix products: 3.52 us -> none  [the longest x3 1.84 us: local(): jax.scipy.linalg.solve_triangular(chol_lower, tall_sketch.T, lower=True)]
  transfers between devices with their start and end apart: 1 -> 0, of which waited for: 1 -> 0; matrix products, arithmetic and copies ran while one was open for 0% -> 0% of each run, Pallas kernels for 0% -> 0%
where the time goes in v1:
time: 54.4 us; the launch traced here: 54.2 us
  Pallas kernels  50.1 us (92%)
  local copies, waits for them, and re-layouts  3.48 us (6%)
  between operations  0.65 us (1%)
    pallas_call x1, Pallas kernels, reduced(): pl.pallas_call(functools.partial(reduce_kernel, modes, a, b), out_shape=j...  35.9 us
    pallas_call x1, Pallas kernels, local(): pl.pallas_call(functools.partial(solve_kernel, math.sqrt(rows * devices))...  14.2 us
    unnamed x6, local copies, waits for them, and re-layouts  3.48 us

profile of v1, /device:TPU:0, one launch (start us, length us, event | category | flops | bytes accessed | tf_op | source)
XLA Modules:
  0.0 54.2 jit_solution(7267629070389182796)
XLA Ops:
  0.6 0.0 copy-start
  0.6 1.2 %copy-done = bf16[1024,512]{1,0:T(8,128)(2,1)S(1)} copy-done((bf16[1024,512]{1,0:T(8,128)(2,1)S(1)}, bf16[1024,512]{1,0:T(8,128)(2,1)}, u32[]{:S(2)}) %copy-start) | copy-done | bytes 1048600
  1.9 0.0 copy-start.1
  1.9 1.2 %copy-done.1 = bf16[1024,512]{1,0:T(8,128)(2,1)S(1)} copy-done((bf16[1024,512]{1,0:T(8,128)(2,1)S(1)}, bf16[1024,512]{1,0:T(8,128)(2,1)}, u32[]{:S(2)}) %copy-start.1) | copy-done | bytes 1048600
  3.1 0.0 copy-start.2
  3.1 1.0 %copy-done.2 = bf16[1024,256]{1,0:T(8,128)(2,1)S(1)} copy-done((bf16[1024,256]{1,0:T(8,128)(2,1)S(1)}, bf16[1024,256]{1,0:T(8,128)(2,1)}, u32[]{:S(2)}) %copy-start.2) | copy-done | bytes 524312
  4.1 35.9 %shard_map.50.full = f32[2304,128]{1,0:T(8,128)S(1)} custom-call(bf16[1024,512]{1,0:T(8,128)(2,1)S(1)} %copy-done, bf16[1024,512]{1,0:T(8,128)(2,1)S(1)} %copy-done.1, bf16[1024,256]{1,0:T(8,128)(2,1)S(1)} %copy-done.2), custom_call_target="tpu_custom_call" | custom-call | tf_op jit(solution)/shard_map/pallas_call | solution.py:159
  40.0 14.2 %shard_map.51 = (bf16[1024,256]{1,0:T(8,128)(2,1)}, bf16[1024,256]{1,0:T(8,128)(2,1)}) custom-call(f32[2304,128]{1,0:T(8,128)S(1)} %shard_map.50.full, bf16[1024,512]{1,0:T(8,128)(2,1)S(1)} %copy-done, bf16[1024,512]{1,0:T(8,128)(2,1)S(1)} %copy-done.1), custom_call_target="tpu_custom_call" | custom-call | tf_op jit(solution)/shard_map/pallas_call | solution.py:283
Async XLA Ops:
  0.6 1.2 %copy-start = (bf16[1024,512]{1,0:T(8,128)(2,1)S(1)}, bf16[1024,512]{1,0:T(8,128)(2,1)}, u32[]{:S(2)}) copy-start(bf16[1024,512]{1,0:T(8,128)(2,1)} %left.3) | copy-start | bytes 3145732
  1.9 1.2 %copy-start.1 = (bf16[1024,512]{1,0:T(8,128)(2,1)S(1)}, bf16[1024,512]{1,0:T(8,128)(2,1)}, u32[]{:S(2)}) copy-start(bf16[1024,512]{1,0:T(8,128)(2,1)} %right.3) | copy-start | bytes 3145732
  3.1 1.0 %copy-start.2 = (bf16[1024,256]{1,0:T(8,128)(2,1)S(1)}, bf16[1024,256]{1,0:T(8,128)(2,1)}, u32[]{:S(2)}) copy-start(bf16[1024,256]{1,0:T(8,128)(2,1)} %gauss.1) | copy-start | bytes 1572868

commit v2 on v1

v2 whole, which is shorter than its diff:
```python
import functools
import math

import jax
import jax.numpy as jnp
from jax import lax
from jax.experimental import pallas as pl
from jax.experimental.pallas import tpu as pltpu
from jax.sharding import PartitionSpec as P

MESH = pl.DeviceIdType.MESH
F32 = jnp.float32
BF16 = jnp.bfloat16
B = 128
T = 8
FULL_PARTS = 4
PARTS = 4


def dot(a, b, dims, precision=None):
    return lax.dot_general(a, b, (dims, ((), ())), precision=precision, preferred_element_type=F32)


def block_list(rank, target):
    n, k = rank // B, target // B
    sketch = [(0, i, j) for i in range(n) for j in range(k)]
    gram = [(1, i, j) for i in range(n) for j in range(i, n)]
    return sketch + gram


def plan(rank, target, modes):
    devices = 2 * modes
    unit = devices * T
    streams, row, counts = [], 0, []
    for kind in (0, 1):
        rows = B * sum(blk[0] == kind for blk in block_list(rank, target))
        units = -(-rows // unit)
        parts = [p for p in (units // 2, units - units // 2) if p]
        counts.append(len(parts))
        for index, part in enumerate(parts):
            streams.append((row, part * T, index == 0))
            row += part * unit
    return streams, counts, row


def first_rows(rank, target, modes):
    streams, counts, _ = plan(rank, target, modes)
    starts = (0, streams[counts[0]][0])
    seen, out = [0, 0], []
    for kind, _, _ in block_list(rank, target):
        out.append(starts[kind] + seen[kind] * B)
        seen[kind] += 1
    return out


def reduce_kernel(modes, left_hbm, right_hbm, gauss_hbm, out, left, right, gauss, buf, full, *rest):
    nz = modes // 4
    rank, target = right.shape[1], gauss.shape[1]
    streams, counts, total = plan(rank, target, modes)
    ns = len(streams)
    recvs = [rest[4 * i:4 * i + 4] for i in range(ns)]
    isem, osem, ssem, rsem, zsend, zrecv = rest[4 * ns:]
    m, c = lax.axis_index("modes"), lax.axis_index("grp")
    x, y, z = m % 2, (m // 2) % 2, m // 4
    core = (m, 1 - c)
    xp = (m + 1 - 2 * x, c)
    yp = (m + 2 - 4 * y, c)
    zs = [((z + k) % nz) for k in range(1, nz)]
    zp = [(x + 2 * y + 4 * t, c) for t in zs]

    rows = right.shape[0]
    loads = []
    for index, (src, dst) in enumerate(((right_hbm, right), (gauss_hbm, gauss), (left_hbm, left))):
        step = rows // PARTS
        for k in range(PARTS):
            cp = pltpu.make_async_copy(src.at[pl.ds(k * step, step), :], dst.at[pl.ds(k * step, step), :], isem.at[index, k])
            cp.start()
            loads.append(cp)

    barrier = pltpu.get_barrier_semaphore()
    partners = [core, xp, yp] + zp
    for p in partners:
        pl.semaphore_signal(barrier, inc=1, device_id=p, device_id_type=MESH)

    starts = first_rows(rank, target, modes)
    where = {blk: row for blk, row in zip(block_list(rank, target), starts)}

    def stream(index):
        off, p, x_first = streams[index]
        r0, r1, r2, rz = recvs[index]
        q = nz * p
        f, s = (x, y) if x_first else (y, x)
        fp, sp = (xp, yp) if x_first else (yp, xp)
        b0 = off + c * 4 * q
        b1 = b0 + f * 2 * q
        b2 = b1 + s * q

        def at(ref, start, size):
            return ref.at[pl.ds(pl.multiple_of(start, T), size), :]

        def send(src, dst, k, dev):
            cp = pltpu.make_async_remote_copy(
                src_ref=src, dst_ref=dst, send_sem=ssem.at[index, k], recv_sem=rsem.at[index, k],
                device_id=dev, device_id_type=MESH)
            cp.start()
            return cp

        def share(start, size, k, dev):
            return send(at(full, start, size), at(full, start, size), k, dev)

        def add(start, size, other):
            i = pl.ds(pl.multiple_of(start, T), size)
            buf[i, :] = buf[i, :] + other[...]

        cp = send(at(buf, off + (1 - c) * 4 * q, 4 * q), r0, 0, core)
        yield
        cp.wait()
        add(b0 + (1 - f) * 2 * q, 2 * q, r0.at[pl.ds(pl.multiple_of((1 - f) * 2 * q, T), 2 * q), :])
        cp = send(at(buf, b0 + (1 - f) * 2 * q, 2 * q), r1, 1, fp)
        add(b1, 2 * q, r0.at[pl.ds(pl.multiple_of(f * 2 * q, T), 2 * q), :])
        yield
        cp.wait()
        add(b1 + (1 - s) * q, q, r1.at[pl.ds(pl.multiple_of((1 - s) * q, T), q), :])
        cp = send(at(buf, b1 + (1 - s) * q, q), r2, 2, sp)
        add(b2, q, r1.at[pl.ds(pl.multiple_of(s * q, T), q), :])
        yield
        cp.wait()
        add(b2, q, r2)
        cps = []
        for k in range(nz - 1):
            cp = pltpu.make_async_remote_copy(
                src_ref=at(buf, b2 + zs[k] * p, p), dst_ref=rz.at[k], send_sem=zsend.at[index, 0, k],
                recv_sem=zrecv.at[index, 0, k], device_id=zp[k], device_id_type=MESH)
            cp.start()
            cps.append(cp)
        yield
        piece = pl.ds(pl.multiple_of(b2 + z * p, T), p)
        acc = buf[piece, :]
        for k in range(nz - 1):
            cps[k].wait()
            acc = acc + rz[k]
        full[piece, :] = acc
        cps = []
        for k in range(nz - 1):
            cp = pltpu.make_async_remote_copy(
                src_ref=full.at[piece, :], dst_ref=full.at[piece, :], send_sem=zsend.at[index, 1, k],
                recv_sem=zrecv.at[index, 1, k], device_id=zp[k], device_id_type=MESH)
            cp.start()
            cps.append(cp)
        yield
        for cp in cps:
            cp.wait()
        c3 = share(b2, q, 3, sp)
        c4 = share(b2, q, 4, fp)
        c5 = share(b2, q, 5, core)
        yield
        c3.wait()
        o2 = b1 + (1 - s) * q
        c6 = share(o2, q, 6, fp)
        c7 = share(o2, q, 7, core)
        yield
        c4.wait()
        c8 = share(b0 + (1 - f) * 2 * q + s * q, q, 8, core)
        yield
        c6.wait()
        c9 = share(b0 + (1 - f) * 2 * q + (1 - s) * q, q, 9, core)
        mine = pltpu.make_async_copy(at(full, b0, 4 * q), at(out, b0, 4 * q), osem.at[index, 0])
        mine.start()
        yield
        for cp in (c5, c7, c8, c9):
            cp.wait()
        theirs = off + (1 - c) * 4 * q
        other = pltpu.make_async_copy(at(full, theirs, 4 * q), at(out, theirs, 4 * q), osem.at[index, 1])
        other.start()
        yield
        mine.wait()
        other.wait()

    for cp in loads[:2 * PARTS]:
        cp.wait()
    sketch = dot(right[...], gauss[...], ((0,), (0,)))
    for (kind, i, j), row in where.items():
        if kind == 0:
            buf[row:row + B, :] = sketch[i * B:(i + 1) * B, j * B:(j + 1) * B]
    end = max(starts) + B
    gram_start = streams[counts[0]][0]
    pad = B * sum(k == 0 for k, _, _ in where)
    if pad < gram_start:
        buf[pad:gram_start, :] = jnp.zeros((gram_start - pad, B), F32)
    if end < total:
        buf[end:, :] = jnp.zeros((total - end, B), F32)
    pl.semaphore_wait(barrier, len(partners))

    active = [stream(i) for i in range(counts[0])]
    for g in active:
        next(g)
    for cp in loads[2 * PARTS:]:
        cp.wait()
    step = 2 * B if rank % (2 * B) == 0 else B
    for r in range(0, rank, step):
        g = dot(left[:, r:r + step], left[:, r:], ((0,), (0,)))
        for i in range(r // B, (r + step) // B):
            for j in range(i, rank // B):
                row = where[(1, i, j)]
                buf[row:row + B, :] = g[i * B - r:(i + 1) * B - r, j * B - r:(j + 1) * B - r]
    late = [stream(counts[0] + i) for i in range(counts[1])]
    for g in late:
        next(g)
    active = active + late
    while active:
        active = [g for g in active if next(g, 0) != 0]


def reduced(left, right, gauss):
    modes = lax.axis_size("modes")
    rows, rank = right.shape
    target = gauss.shape[1]
    streams, _, total = plan(rank, target, modes)
    nz = modes // 4
    dma = pltpu.SemaphoreType.DMA
    landing = []
    for _, p, _ in streams:
        q = nz * p
        landing += [pltpu.VMEM((4 * q, B), F32), pltpu.VMEM((2 * q, B), F32), pltpu.VMEM((q, B), F32), pltpu.VMEM((nz - 1, p, B), F32)]
    return pl.pallas_call(
        functools.partial(reduce_kernel, modes),
        out_shape=jax.ShapeDtypeStruct((total, B), F32),
        in_specs=[pl.BlockSpec(memory_space=pl.ANY)] * 3,
        out_specs=pl.BlockSpec(memory_space=pl.ANY),
        scratch_shapes=[
            pltpu.VMEM((rows, rank), BF16),
            pltpu.VMEM((rows, rank), BF16),
            pltpu.VMEM((rows, target), BF16),
            pltpu.VMEM((total, B), F32),
            pltpu.VMEM((total, B), F32),
            *landing,
            dma((3, PARTS)),
            dma((len(streams), 2)),
            dma((len(streams), 10)),
            dma((len(streams), 10)),
            dma((len(streams), 2, nz - 1)),
            dma((len(streams), 2, nz - 1)),
        ],
        compiler_params=pltpu.CompilerParams(collective_id=0, has_side_effects=True, vmem_limit_bytes=61 << 20),
    )(left, right, gauss)


def factor_inverse(block, spl, rowbuf):
    n = B // T
    row = lax.broadcasted_iota(jnp.int32, (T, B), 0)
    lane = lax.broadcasted_iota(jnp.int32, (T, B), 1)
    A = [block[t * T:(t + 1) * T, :] for t in range(n)]
    M = [(row + t * T == lane).astype(F32) for t in range(n)]
    out = []
    for p in range(n):
        k0 = p * T
        for j in range(T):
            spl[p % 2, j] = jnp.broadcast_to(A[p][:, k0 + j:k0 + j + 1], (T, B))
        s = [[jnp.broadcast_to(spl[p % 2, j, i:i + 1, :], (T, B)) if j <= i else None for j in range(T)] for i in range(T)]
        w = [[None] * T for _ in range(T)]
        rs, rd = [], []
        for k in range(T):
            r = lax.rsqrt(s[k][k])
            rs.append(r)
            rd.append(r * r)
            for i in range(k + 1, T):
                w[i][k] = s[i][k] * rd[k]
            for j in range(k + 1, T):
                for i in range(j, T):
                    s[i][j] = s[i][j] - w[i][k] * s[j][k]
        rowbuf[p % 2, 0] = A[p]
        rowbuf[p % 2, 1] = M[p]
        xa = [jnp.broadcast_to(rowbuf[p % 2, 0, i:i + 1, :], (T, B)) for i in range(T)]
        xm = [jnp.broadcast_to(rowbuf[p % 2, 1, i:i + 1, :], (T, B)) for i in range(T)]
        for k in range(T):
            for i in range(k + 1, T):
                xa[i] = xa[i] - w[i][k] * xa[k]
                xm[i] = xm[i] - w[i][k] * xm[k]
        o = xm[0] * rs[0]
        for i in range(1, T):
            o = jnp.where(row == i, xm[i] * rs[i], o)
        out.append(o)
        if p + 1 == n:
            break
        va = [xa[i] * rd[i] for i in range(T)]
        vm = [xm[i] * rd[i] for i in range(T)]
        for k in range(T - 1, 0, -1):
            for i in range(k):
                va[i] = va[i] - w[k][i] * va[k]
                vm[i] = vm[i] - w[k][i] * vm[k]
        for t in range(p + 1, n):
            da = dm = None
            for j in range(T):
                cj = jnp.broadcast_to(A[t][:, k0 + j:k0 + j + 1], (T, B))
                da = cj * va[j] if da is None else da + cj * va[j]
                dm = cj * vm[j] if dm is None else dm + cj * vm[j]
            A[t] = A[t] - da
            M[t] = M[t] - dm
    return jnp.concatenate(out, axis=0)


def halves(v):
    hi = v.astype(BF16)
    return hi, (v - hi.astype(F32)).astype(BF16)


def solve_kernel(scale, modes, full_hbm, left_hbm, right_hbm, left_new, right_new, full, left, right, lout, rout, sk, gm, spl, rowbuf, fsem, isem, osem):
    high = lax.Precision.HIGHEST
    rows, rank, target = left.shape[0], left.shape[1], lout.shape[1]
    step = rows // PARTS
    parts = [pl.ds(k * step, step) for k in range(PARTS)]
    blocks = list(zip(block_list(rank, target), first_rows(rank, target, modes)))
    chunk = full.shape[0] // FULL_PARTS
    gets = []
    for k in range(FULL_PARTS):
        cp = pltpu.make_async_copy(full_hbm.at[pl.ds(k * chunk, chunk), :], full.at[pl.ds(k * chunk, chunk), :], fsem.at[k])
        cp.start()
        gets.append(cp)
    loads = []
    for index, (src, dst) in enumerate(((left_hbm, left), (right_hbm, right))):
        for k, part in enumerate(parts):
            cp = pltpu.make_async_copy(src.at[part, :], dst.at[part, :], isem.at[index, k])
            cp.start()
            loads.append(cp)
    for cp in gets:
        cp.wait()
    for (kind, i, j), pos in blocks:
        v = full[pos:pos + B, :]
        if kind == 0:
            sk[j * B:(j + 1) * B, i * B:(i + 1) * B] = v.T
        else:
            gm[i * B:(i + 1) * B, j * B:(j + 1) * B] = v
            if i != j:
                gm[j * B:(j + 1) * B, i * B:(i + 1) * B] = v.T
    nn, nt = ((1,), (0,)), ((1,), (1,))
    st = sk[...]
    cross = dot(st, gm[...], nn, high)
    gram = dot(cross, st, nt, high)
    nb = target // B
    low, inv = [], []
    for r in range(nb):
        diag = gram[r * B:(r + 1) * B, r * B:(r + 1) * B]
        if r:
            prev = inv[0] if r == 1 else jnp.concatenate(inv, axis=0)
            lr = dot(gram[r * B:(r + 1) * B, :r * B], prev, nt, high)
            diag = diag - dot(lr, lr, nt, high)
        mi = factor_inverse(diag, spl, rowbuf)
        if r:
            rest = -dot(mi, dot(lr, prev, nn, high), nn, high)
            mi = jnp.concatenate([rest, mi], axis=1)
            inv = [jnp.concatenate([v, jnp.zeros((B, B), F32)], axis=1) for v in inv]
        inv.append(mi)
    inverse = inv[0] if nb == 1 else jnp.concatenate(inv, axis=0)
    wh, wl = halves(dot(inverse, st, nn, high) * scale)
    ph, plo = halves(dot(inverse, cross, nn, high) * (1.0 / scale))
    for cp in loads:
        cp.wait()
    stores = []
    for index, (src, hi, lo, out, dst) in enumerate(((left, wh, wl, lout, left_new), (right, ph, plo, rout, right_new))):
        for k, part in enumerate(parts):
            v = src[part, :]
            out[part, :] = (dot(v, hi, nt) + dot(v, lo, nt)).astype(BF16)
            cp = pltpu.make_async_copy(out.at[part, :], dst.at[part, :], osem.at[index, k])
            cp.start()
            stores.append(cp)
    for cp in stores:
        cp.wait()


def local(left_core, right_core, gauss_core):
    rows, rank = left_core.shape
    target = gauss_core.shape[1]
    devices = lax.axis_size("modes") * lax.axis_size("grp")
    full = reduced(left_core, right_core, gauss_core)
    out = jax.ShapeDtypeStruct((rows, target), BF16)
    return pl.pallas_call(
        functools.partial(solve_kernel, math.sqrt(rows * devices), lax.axis_size("modes")),
        out_shape=(out, out),
        in_specs=[pl.BlockSpec(memory_space=pl.ANY)] * 3,
        out_specs=(pl.BlockSpec(memory_space=pl.ANY),) * 2,
        scratch_shapes=[
            pltpu.VMEM(full.shape, F32),
            pltpu.VMEM((rows, rank), BF16),
            pltpu.VMEM((rows, rank), BF16),
            pltpu.VMEM((rows, target), BF16),
            pltpu.VMEM((rows, target), BF16),
            pltpu.VMEM((target, rank), F32),
            pltpu.VMEM((rank, rank), F32),
            pltpu.VMEM((2, T, T, B), F32),
            pltpu.VMEM((2, 2, T, B), F32),
            pltpu.SemaphoreType.DMA((FULL_PARTS,)),
            pltpu.SemaphoreType.DMA((2, PARTS)),
            pltpu.SemaphoreType.DMA((2, PARTS)),
        ],
        compiler_params=pltpu.CompilerParams(vmem_limit_bytes=61 << 20),
    )(full, left_core, right_core)


def solution(mesh):
    spec = P(("modes", "grp"), None)
    return jax.shard_map(local, mesh=mesh, in_specs=(spec,) * 3, out_specs=(spec, spec), check_vma=False)
```

time: 54.4 us -> 48.8 us (0.90)
  local copies, waits for them, and re-layouts: 3.48 us -> 0 us
  Pallas kernels: 50.1 us -> 48 us
    unnamed x6 -> x0, local copies, waits for them, and re-layouts: 3.48 us -> none
    pallas_call x2, Pallas kernels: 50.1 us -> 48 us  [the longest x1 32 us: reduced(): pl.pallas_call(functools.partial(reduce_kernel, modes), out_shape=jax.Sha...]
where the time goes in v2:
time: 48.8 us; the launch traced here: 48.6 us
  Pallas kernels  48 us (98%)
  between operations  0.64 us (1%)
    pallas_call x1, Pallas kernels, reduced(): pl.pallas_call(functools.partial(reduce_kernel, modes), out_shape=jax.Sha...  32 us
    pallas_call x1, Pallas kernels, local(): pl.pallas_call(functools.partial(solve_kernel, math.sqrt(rows * devices),...  16 us

profile of v2, /device:TPU:0, one launch (start us, length us, event | category | flops | bytes accessed | tf_op | source)
XLA Modules:
  0.0 48.6 jit_solution(7321699146282490866)
XLA Ops:
  0.6 32.0 %shard_map.50.full_hbm = f32[2304,128]{1,0:T(8,128)} custom-call(bf16[1024,512]{1,0:T(8,128)(2,1)} %left_hbm.3, bf16[1024,512]{1,0:T(8,128)(2,1)} %right_hbm.3, bf16[1024,256]{1,0:T(8,128)(2,1)} %gauss_hbm.1), custom_call_target="tpu_custom_call" | custom-call | tf_op jit(solution)/shard_map/pallas_call | solution.py:225
  32.6 16.0 %shard_map.51 = (bf16[1024,256]{1,0:T(8,128)(2,1)}, bf16[1024,256]{1,0:T(8,128)(2,1)}) custom-call(f32[2304,128]{1,0:T(8,128)} %shard_map.50.full_hbm, bf16[1024,512]{1,0:T(8,128)(2,1)} %left_hbm.3, bf16[1024,512]{1,0:T(8,128)(2,1)} %right_hbm.3), custom_call_target="tpu_custom_call" | custom-call | tf_op jit(solution)/shard_map/pallas_call | solution.py:376

commit v3 on v2

--- a/solution.py
+++ b/solution.py
@@ -28,6 +28,9 @@
     return sketch + gram
 
 
+ORDERS = (((0, 1, 2), (1, 2, 0)), ((2, 0, 1), (0, 1, 2), (1, 0, 2)))
+
+
 def plan(rank, target, modes):
     devices = 2 * modes
     unit = devices * T
@@ -35,11 +38,15 @@
     for kind in (0, 1):
         rows = B * sum(blk[0] == kind for blk in block_list(rank, target))
         units = -(-rows // unit)
-        parts = [p for p in (units // 2, units - units // 2) if p]
-        counts.append(len(parts))
-        for index, part in enumerate(parts):
-            streams.append((row, part * T, index == 0))
-            row += part * unit
+        ways = len(ORDERS[kind])
+        count = 0
+        for index in range(ways):
+            part = (units + ways - 1 - index) // ways
+            if part:
+                streams.append((row, part * T, ORDERS[kind][index] + tuple(range(3, modes.bit_length() - 1))))
+                row += part * unit
+                count += 1
+        counts.append(count)
     return streams, counts, row
 
 
@@ -54,19 +61,15 @@
 
 
 def reduce_kernel(modes, left_hbm, right_hbm, gauss_hbm, out, left, right, gauss, buf, full, *rest):
-    nz = modes // 4
     rank, target = right.shape[1], gauss.shape[1]
     streams, counts, total = plan(rank, target, modes)
     ns = len(streams)
-    recvs = [rest[4 * i:4 * i + 4] for i in range(ns)]
-    isem, osem, ssem, rsem, zsend, zrecv = rest[4 * ns:]
+    landings = rest[:ns]
+    isem, osem, ssem, rsem = rest[ns:]
     m, c = lax.axis_index("modes"), lax.axis_index("grp")
-    x, y, z = m % 2, (m // 2) % 2, m // 4
     core = (m, 1 - c)
-    xp = (m + 1 - 2 * x, c)
-    yp = (m + 2 - 4 * y, c)
-    zs = [((z + k) % nz) for k in range(1, nz)]
-    zp = [(x + 2 * y + 4 * t, c) for t in zs]
+    bits = [(m // 2**k) % 2 for k in range(modes.bit_length() - 1)]
+    across = [(m + (1 - 2 * v) * 2**k, c) for k, v in enumerate(bits)]
 
     rows = right.shape[0]
     loads = []
@@ -78,99 +81,65 @@
             loads.append(cp)
 
     barrier = pltpu.get_barrier_semaphore()
-    partners = [core, xp, yp] + zp
+    partners = [core] + across
     for p in partners:
         pl.semaphore_signal(barrier, inc=1, device_id=p, device_id_type=MESH)
 
     starts = first_rows(rank, target, modes)
     where = {blk: row for blk, row in zip(block_list(rank, target), starts)}
 
+    sems = ssem.shape[1]
+
     def stream(index):
-        off, p, x_first = streams[index]
-        r0, r1, r2, rz = recvs[index]
-        q = nz * p
-        f, s = (x, y) if x_first else (y, x)
-        fp, sp = (xp, yp) if x_first else (yp, xp)
-        b0 = off + c * 4 * q
-        b1 = b0 + f * 2 * q
-        b2 = b1 + s * q
+        off, p, order = streams[index]
+        landing = landings[index]
+        count = iter(range(sems))
 
         def at(ref, start, size):
             return ref.at[pl.ds(pl.multiple_of(start, T), size), :]
 
-        def send(src, dst, k, dev):
+        def send(src, dst, dev):
+            k = next(count)
             cp = pltpu.make_async_remote_copy(
                 src_ref=src, dst_ref=dst, send_sem=ssem.at[index, k], recv_sem=rsem.at[index, k],
                 device_id=dev, device_id_type=MESH)
             cp.start()
             return cp
 
-        def share(start, size, k, dev):
-            return send(at(full, start, size), at(full, start, size), k, dev)
-
-        def add(start, size, other):
-            i = pl.ds(pl.multiple_of(start, T), size)
-            buf[i, :] = buf[i, :] + other[...]
-
-        cp = send(at(buf, off + (1 - c) * 4 * q, 4 * q), r0, 0, core)
-        yield
-        cp.wait()
-        add(b0 + (1 - f) * 2 * q, 2 * q, r0.at[pl.ds(pl.multiple_of((1 - f) * 2 * q, T), 2 * q), :])
-        cp = send(at(buf, b0 + (1 - f) * 2 * q, 2 * q), r1, 1, fp)
-        add(b1, 2 * q, r0.at[pl.ds(pl.multiple_of(f * 2 * q, T), 2 * q), :])
-        yield
-        cp.wait()
-        add(b1 + (1 - s) * q, q, r1.at[pl.ds(pl.multiple_of((1 - s) * q, T), q), :])
-        cp = send(at(buf, b1 + (1 - s) * q, q), r2, 2, sp)
-        add(b2, q, r1.at[pl.ds(pl.multiple_of(s * q, T), q), :])
-        yield
-        cp.wait()
-        add(b2, q, r2)
-        cps = []
-        for k in range(nz - 1):
-            cp = pltpu.make_async_remote_copy(
-                src_ref=at(buf, b2 + zs[k] * p, p), dst_ref=rz.at[k], send_sem=zsend.at[index, 0, k],
-                recv_sem=zrecv.at[index, 0, k], device_id=zp[k], device_id_type=MESH)
-            cp.start()
-            cps.append(cp)
-        yield
-        piece = pl.ds(pl.multiple_of(b2 + z * p, T), p)
-        acc = buf[piece, :]
-        for k in range(nz - 1):
-            cps[k].wait()
-            acc = acc + rz[k]
-        full[piece, :] = acc
-        cps = []
-        for k in range(nz - 1):
-            cp = pltpu.make_async_remote_copy(
-                src_ref=full.at[piece, :], dst_ref=full.at[piece, :], send_sem=zsend.at[index, 1, k],
-                recv_sem=zrecv.at[index, 1, k], device_id=zp[k], device_id_type=MESH)
-            cp.start()
-            cps.append(cp)
-        yield
-        for cp in cps:
+        def share(start, size, dev):
+            return send(at(full, start, size), at(full, start, size), dev)
+
+        size, base, free = 2 * p * modes, off, 0
+        for step, (v, dev) in enumerate([(c, core)] + [(bits[k], across[k]) for k in order]):
+            size //= 2
+            got = landing.at[pl.ds(free, size), :]
+            free += size
+            cp = send(at(buf, base + (1 - v) * size, size), got, dev)
+            yield
             cp.wait()
-        c3 = share(b2, q, 3, sp)
-        c4 = share(b2, q, 4, fp)
-        c5 = share(b2, q, 5, core)
-        yield
-        c3.wait()
-        o2 = b1 + (1 - s) * q
-        c6 = share(o2, q, 6, fp)
-        c7 = share(o2, q, 7, core)
-        yield
-        c4.wait()
-        c8 = share(b0 + (1 - f) * 2 * q + s * q, q, 8, core)
-        yield
-        c6.wait()
-        c9 = share(b0 + (1 - f) * 2 * q + (1 - s) * q, q, 9, core)
-        mine = pltpu.make_async_copy(at(full, b0, 4 * q), at(out, b0, 4 * q), osem.at[index, 0])
+            base = base + v * size
+            i = pl.ds(pl.multiple_of(base, T), size)
+            if step < len(order):
+                buf[i, :] = buf[i, :] + got[...]
+            else:
+                full[i, :] = buf[i, :] + got[...]
+
+        shared = [share(base, size, core)]
+        for k in reversed(order):
+            v = bits[k]
+            cp = share(base, size, across[k])
+            yield
+            cp.wait()
+            shared.append(share(base + (1 - 2 * v) * size, size, core))
+            base = base - v * size
+            size *= 2
+        mine = pltpu.make_async_copy(at(full, base, size), at(out, base, size), osem.at[index, 0])
         mine.start()
         yield
-        for cp in (c5, c7, c8, c9):
+        for cp in shared:
             cp.wait()
-        theirs = off + (1 - c) * 4 * q
-        other = pltpu.make_async_copy(at(full, theirs, 4 * q), at(out, theirs, 4 * q), osem.at[index, 1])
+        theirs = off + (1 - c) * size
+        other = pltpu.make_async_copy(at(full, theirs, size), at(out, theirs, size), osem.at[index, 1])
         other.start()
         yield
         mine.wait()
@@ -216,12 +185,9 @@
     rows, rank = right.shape
     target = gauss.shape[1]
     streams, _, total = plan(rank, target, modes)
-    nz = modes // 4
     dma = pltpu.SemaphoreType.DMA
-    landing = []
-    for _, p, _ in streams:
-        q = nz * p
-        landing += [pltpu.VMEM((4 * q, B), F32), pltpu.VMEM((2 * q, B), F32), pltpu.VMEM((q, B), F32), pltpu.VMEM((nz - 1, p, B), F32)]
+    landing = [pltpu.VMEM((2 * p * modes, B), F32) for _, p, _ in streams]
+    sems = 3 * modes.bit_length()
     return pl.pallas_call(
         functools.partial(reduce_kernel, modes),
         out_shape=jax.ShapeDtypeStruct((total, B), F32),
@@ -236,10 +202,8 @@
             *landing,
             dma((3, PARTS)),
             dma((len(streams), 2)),
-            dma((len(streams), 10)),
-            dma((len(streams), 10)),
-            dma((len(streams), 2, nz - 1)),
-            dma((len(streams), 2, nz - 1)),
+            dma((len(streams), sems)),
+            dma((len(streams), sems)),
         ],
         compiler_params=pltpu.CompilerParams(collective_id=0, has_side_effects=True, vmem_limit_bytes=61 << 20),
     )(left, right, gauss)
@@ -304,6 +268,13 @@
     return hi, (v - hi.astype(F32)).astype(BF16)
 
 
+def product(a, b):
+    ah, al = halves(a)
+    bh, bl = halves(b)
+    nn = ((1,), (0,))
+    return dot(ah, bh, nn) + (dot(ah, bl, nn) + dot(al, bh, nn))
+
+
 def solve_kernel(scale, modes, full_hbm, left_hbm, right_hbm, left_new, right_new, full, left, right, lout, rout, sk, gm, spl, rowbuf, fsem, isem, osem):
     high = lax.Precision.HIGHEST
     rows, rank, target = left.shape[0], left.shape[1], lout.shape[1]
@@ -316,14 +287,14 @@
         cp = pltpu.make_async_copy(full_hbm.at[pl.ds(k * chunk, chunk), :], full.at[pl.ds(k * chunk, chunk), :], fsem.at[k])
         cp.start()
         gets.append(cp)
+    for cp in gets:
+        cp.wait()
     loads = []
     for index, (src, dst) in enumerate(((left_hbm, left), (right_hbm, right))):
         for k, part in enumerate(parts):
             cp = pltpu.make_async_copy(src.at[part, :], dst.at[part, :], isem.at[index, k])
             cp.start()
             loads.append(cp)
-    for cp in gets:
-        cp.wait()
     for (kind, i, j), pos in blocks:
         v = full[pos:pos + B, :]
         if kind == 0:
@@ -351,8 +322,8 @@
             inv = [jnp.concatenate([v, jnp.zeros((B, B), F32)], axis=1) for v in inv]
         inv.append(mi)
     inverse = inv[0] if nb == 1 else jnp.concatenate(inv, axis=0)
-    wh, wl = halves(dot(inverse, st, nn, high) * scale)
-    ph, plo = halves(dot(inverse, cross, nn, high) * (1.0 / scale))
+    wh, wl = halves(product(inverse, st) * scale)
+    ph, plo = halves(product(inverse, cross) * (1.0 / scale))
     for cp in loads:
         cp.wait()
     stores = []

time: 48.8 us -> 50.9 us (1.043)
  Pallas kernels: 48 us -> 50.1 us
    pallas_call x1, Pallas kernels: 32 us -> 35.1 us  [reduced(): pl.pallas_call(functools.partial(reduce_kernel, modes), out_shape=jax.Sha...]
    pallas_call x1, Pallas kernels: 16 us -> 15 us  [local(): pl.pallas_call(functools.partial(solve_kernel, math.sqrt(rows * devices),...]
where the time goes in v3:
time: 50.9 us; the launch traced here: 50.7 us
  Pallas kernels  50.1 us (98%)
  between operations  0.64 us (1%)
    pallas_call x1, Pallas kernels, reduced(): pl.pallas_call(functools.partial(reduce_kernel, modes), out_shape=jax.Sha...  35.1 us
    pallas_call x1, Pallas kernels, local(): pl.pallas_call(functools.partial(solve_kernel, math.sqrt(rows * devices),...  15 us

profile of v3, /device:TPU:0, one launch (start us, length us, event | category | flops | bytes accessed | tf_op | source)
XLA Modules:
  0.0 50.7 jit_solution(14029336699791699228)
XLA Ops:
  0.6 35.1 %shard_map.50.full_hbm = f32[2304,128]{1,0:T(8,128)} custom-call(bf16[1024,512]{1,0:T(8,128)(2,1)} %left_hbm.3, bf16[1024,512]{1,0:T(8,128)(2,1)} %right_hbm.3, bf16[1024,256]{1,0:T(8,128)(2,1)} %gauss_hbm.1), custom_call_target="tpu_custom_call" | custom-call | tf_op jit(solution)/shard_map/pallas_call | solution.py:191
  35.7 15.0 %shard_map.51 = (bf16[1024,256]{1,0:T(8,128)(2,1)}, bf16[1024,256]{1,0:T(8,128)(2,1)}) custom-call(f32[2304,128]{1,0:T(8,128)} %shard_map.50.full_hbm, bf16[1024,512]{1,0:T(8,128)(2,1)} %left_hbm.3, bf16[1024,512]{1,0:T(8,128)(2,1)} %right_hbm.3), custom_call_target="tpu_custom_call" | custom-call | tf_op jit(solution)/shard_map/pallas_call | solution.py:347

commit v4 on v2

--- a/solution.py
+++ b/solution.py
@@ -304,6 +304,13 @@
     return hi, (v - hi.astype(F32)).astype(BF16)
 
 
+def product(a, b):
+    ah, al = halves(a)
+    bh, bl = halves(b)
+    nn = ((1,), (0,))
+    return dot(ah, bh, nn) + (dot(ah, bl, nn) + dot(al, bh, nn))
+
+
 def solve_kernel(scale, modes, full_hbm, left_hbm, right_hbm, left_new, right_new, full, left, right, lout, rout, sk, gm, spl, rowbuf, fsem, isem, osem):
     high = lax.Precision.HIGHEST
     rows, rank, target = left.shape[0], left.shape[1], lout.shape[1]
@@ -316,14 +323,14 @@
         cp = pltpu.make_async_copy(full_hbm.at[pl.ds(k * chunk, chunk), :], full.at[pl.ds(k * chunk, chunk), :], fsem.at[k])
         cp.start()
         gets.append(cp)
+    for cp in gets:
+        cp.wait()
     loads = []
     for index, (src, dst) in enumerate(((left_hbm, left), (right_hbm, right))):
         for k, part in enumerate(parts):
             cp = pltpu.make_async_copy(src.at[part, :], dst.at[part, :], isem.at[index, k])
             cp.start()
             loads.append(cp)
-    for cp in gets:
-        cp.wait()
     for (kind, i, j), pos in blocks:
         v = full[pos:pos + B, :]
         if kind == 0:
@@ -351,8 +358,8 @@
             inv = [jnp.concatenate([v, jnp.zeros((B, B), F32)], axis=1) for v in inv]
         inv.append(mi)
     inverse = inv[0] if nb == 1 else jnp.concatenate(inv, axis=0)
-    wh, wl = halves(dot(inverse, st, nn, high) * scale)
-    ph, plo = halves(dot(inverse, cross, nn, high) * (1.0 / scale))
+    wh, wl = halves(product(inverse, st) * scale)
+    ph, plo = halves(product(inverse, cross) * (1.0 / scale))
     for cp in loads:
         cp.wait()
     stores = []

time: 48.8 us -> 47.8 us (0.980)
  Pallas kernels: 48 us -> 47 us
    pallas_call x1, Pallas kernels: 16 us -> 15 us  [local(): pl.pallas_call(functools.partial(solve_kernel, math.sqrt(rows * devices),...]
where the time goes in v4:
time: 47.8 us; the launch traced here: 47.6 us
  Pallas kernels  47 us (98%)
  between operations  0.64 us (1%)
    pallas_call x1, Pallas kernels, reduced(): pl.pallas_call(functools.partial(reduce_kernel, modes), out_shape=jax.Sha...  32 us
    pallas_call x1, Pallas kernels, local(): pl.pallas_call(functools.partial(solve_kernel, math.sqrt(rows * devices),...  15 us

profile of v4, /device:TPU:0, one launch (start us, length us, event | category | flops | bytes accessed | tf_op | source)
XLA Modules:
  0.0 47.6 jit_solution(13025957761453091755)
XLA Ops:
  0.6 32.0 %shard_map.50.full_hbm = f32[2304,128]{1,0:T(8,128)} custom-call(bf16[1024,512]{1,0:T(8,128)(2,1)} %left_hbm.3, bf16[1024,512]{1,0:T(8,128)(2,1)} %right_hbm.3, bf16[1024,256]{1,0:T(8,128)(2,1)} %gauss_hbm.1), custom_call_target="tpu_custom_call" | custom-call | tf_op jit(solution)/shard_map/pallas_call | solution.py:225
  32.6 15.0 %shard_map.51 = (bf16[1024,256]{1,0:T(8,128)(2,1)}, bf16[1024,256]{1,0:T(8,128)(2,1)}) custom-call(f32[2304,128]{1,0:T(8,128)} %shard_map.50.full_hbm, bf16[1024,512]{1,0:T(8,128)(2,1)} %left_hbm.3, bf16[1024,512]{1,0:T(8,128)(2,1)} %right_hbm.3), custom_call_target="tpu_custom_call" | custom-call | tf_op jit(solution)/shard_map/pallas_call | solution.py:383
